TPU v7x, 128 devices: a whole 4x4x4 slice. The times are simulated.
128 devices in a mesh: cand: 8 (over y, core), hist: 16 (over z, x).
Axes of the slice: x: 4, y: 4, z: 4, core: 2. Of those that a mesh axis runs over, the one named last changes fastest.
Arguments:
- cand_x: bfloat16 [512, 128, 1024], P(('cand', 'hist')), may hold values from -6 to 6
- w_query: bfloat16 [1024, 1024], replicated, may hold values from -0.1875 to 0.1875
- w_gate: bfloat16 [1024, 1024], replicated, may hold values from -0.1875 to 0.1875
- w_out: bfloat16 [1024, 1024], replicated, may hold values from -0.1875 to 0.1875
- history_kv: bfloat16 [16, 48, 128, 2048], P('cand', 'hist')
- tile_user: int32 [512], P('cand'), may hold values from 0 to 15, as said below
- user_row: int32 [16], replicated, may hold values from 0 to 15, as said below
- hist_len: int32 [16], replicated, may hold values from 1 to 6144, as said below
- pattern: int32 [512, 48], P('cand', 'hist'), may hold values 0 or 1
Outputs:
- mixed: bfloat16 [512, 128, 1024], P(('cand', 'hist'))
Inputs may be any that keep to these rules, and one draw needn't show every extreme that they name: `tile_user`: the tiles of each index of cand (64 consecutive tiles) name, among the 2 cache rows of each index of cand (rows k * 2 to k * 2 + 1 for index k), exactly 1. `user_row`: each cache row is used by exactly one user. `hist_len`: some user has exactly 6144 actions.
All inputs are finite; a program needn't handle non-finite values. No bound on the sum of `pattern` on one device may be relied on, other than what follows from the above.
Results may differ from a plain program's by a relative error of at most 0.013.
Values may be sent and summed in bfloat16 or wider, within the bound.
A program may use at most 192 MiB of HBM per device.

v0:
```python
import jax
import jax.numpy as jnp
from jax import lax
from jax.sharding import PartitionSpec as P

DH = 128


norm_epsilon = 1e-05


def per_device(cand_x, w_query, w_gate, w_out, history_kv, tile_user, user_row, hist_len, pattern):
    tiles_here, block_len, model_width = cand_x.shape
    flat_rows = cand_x.reshape(tiles_here * block_len, model_width)
    queries = jax.nn.silu(jnp.dot(flat_rows, w_query, preferred_element_type=jnp.float32)).astype(
        jnp.bfloat16
    )
    gate_act = jax.nn.silu(jnp.dot(flat_rows, w_gate, preferred_element_type=jnp.float32)).astype(
        jnp.bfloat16
    )
    head_count = model_width // DH
    queries = queries.reshape(tiles_here, block_len, head_count, DH).transpose(0, 2, 1, 3)
    blocks_here = history_kv.shape[1]
    user_count = user_row.shape[0]
    cache_buffer = lax.all_gather(history_kv, "cand", axis=0, tiled=True)
    slot_rows = jnp.arange(user_count, dtype=jnp.int32)
    slot_count = slot_rows.shape[0]
    span = blocks_here * block_len
    split_cache = cache_buffer.reshape(slot_count, span, 2, head_count, DH)
    key_heads = split_cache[:, :, 0].transpose(0, 2, 1, 3)
    value_heads = split_cache[:, :, 1].transpose(0, 2, 1, 3)
    slot_ids = jnp.arange(slot_count, dtype=jnp.int32)
    first_position = lax.axis_index("hist") * span
    positions = first_position + jnp.arange(span, dtype=jnp.int32)
    score_scale = 1.0 / DH**0.5
    q_tiles = lax.all_gather(queries, "hist", axis=0, tiled=True)
    tile_count = q_tiles.shape[0]
    rows_named = user_row[tile_user]
    slot_index = jnp.sum(
        slot_ids[None, :] * (slot_rows[None, :] == rows_named[:, None]).astype(jnp.int32), axis=1
    )
    lengths = hist_len[tile_user]
    block_open = jnp.broadcast_to(
        pattern[:, :, None], (tile_count, blocks_here, block_len)
    ).reshape(tile_count, span)
    allowed = (positions[None, :] < lengths[:, None]) & (block_open > 0)
    length_float = lengths.astype(jnp.float32)

    def one_tile(tile_item):
        q_tile, slot_one, allowed_row, length_one = tile_item
        key_rows = lax.dynamic_index_in_dim(key_heads, slot_one, 0, keepdims=False)
        value_rows = lax.dynamic_index_in_dim(value_heads, slot_one, 0, keepdims=False)
        scores = (
            jnp.einsum("hcd,htd->hct", q_tile, key_rows, preferred_element_type=jnp.float32)
            * score_scale
        )
        weights = (
            jnp.where(allowed_row[None, None, :], jax.nn.silu(scores), 0.0) / length_one
        ).astype(jnp.bfloat16)
        partial_out = jnp.einsum(
            "hct,htd->chd", weights, value_rows, preferred_element_type=jnp.float32
        )
        return partial_out.reshape(block_len, model_width)

    partial_sums = lax.map(one_tile, (q_tiles, slot_index, allowed, length_float))
    partial_sums = lax.optimization_barrier(partial_sums.astype(jnp.bfloat16)).astype(jnp.float32)
    attention = lax.psum_scatter(
        partial_sums.astype(jnp.bfloat16), "hist", scatter_dimension=0, tiled=True
    ).astype(jnp.float32)
    attention = attention.reshape(tiles_here * block_len, model_width)
    mean_square = jnp.mean(attention * attention, axis=-1, keepdims=True)
    normed = attention * lax.rsqrt(mean_square + norm_epsilon)
    hidden = (normed * gate_act.astype(jnp.float32)).astype(jnp.bfloat16)
    mixed = jnp.dot(hidden, w_out, preferred_element_type=jnp.float32) + flat_rows.astype(
        jnp.float32
    )
    return mixed.astype(jnp.bfloat16).reshape(tiles_here, block_len, model_width)


def solution(mesh):
    return jax.shard_map(
        per_device,
        mesh=mesh,
        in_specs=(
            P(("cand", "hist"), None, None),
            P(),
            P(),
            P(),
            P("cand", "hist", None, None),
            P("cand"),
            P(),
            P(),
            P("cand", "hist"),
        ),
        out_specs=P(("cand", "hist"), None, None),
        check_vma=False,
    )
```

profile of v0, /device:TPU:24, one launch (start us, length us, event | category | flops | bytes accessed | tf_op | source)
XLA Modules:
  0.0 919.4 jit_solution(5546688888534338206)
XLA Ops:
  13.5 116.7 %all-gather.3.cloned.1.call-done = bf16[16,3,128,2048]{3,2,1,0:T(8,128)(2,1)} async-done(((bf16[2,3,128,2048]{3,2,1,0:T(8,128)(2,1)}), bf16[16,3,128,2048]{3,2,1,0:T(8,128)(2,1)}) %all-gather.3.cloned.1.call-update) | async-done | bytes 25165840 | tf_op jit(solution)/shard_map/all_gather | solution.py:25
  130.2 14.2 %copy.31 = bf16[768,8,16,128]{3,2,1,0:T(8,128)(2,1)S(1)} copy(bf16[768,8,16,128]{3,1,2,0:T(8,128)(2,1)} %bitcast.68) | data formatting | bytes 50331648
  144.5 9.5 %slice_bitcast_fusion = (bf16[16,8,384,128]{3,1,2,0:T(8,128)(2,1)}, bf16[16,8,384,128]{3,1,2,0:T(8,128)(2,1)}) fusion(bf16[16,384,2,8,128]{4,3,2,1,0:T(8,128)(2,1)S(1)} %bitcast.67), kind=kLoop, calls=%fused_computation.21 | loop fusion | bytes 50331648 | tf_op jit(solution)/shard_map/transpose | solution.py:30
  153.9 92.1 %all-gather.5.cloned.1.call-done = bf16[64,8,128,128]{3,2,1,0:T(8,128)(2,1)} async-done(((bf16[4,8,128,128]{3,2,1,0:T(8,128)(2,1)}), bf16[64,8,128,128]{3,2,1,0:T(8,128)(2,1)}) %all-gather.5.cloned.1.call-update) | async-done | bytes 16777232 | tf_op jit(solution)/shard_map/all_gather | solution.py:36
  246.1 547.8 %while.10 = (s32[]{:T(128)}, bf16[64,128,1024]{1,2,0:T(8,128)(2,1)}, s32[64]{0:T(128)S(1)}, bf16[16,8,384,128]{3,1,2,0:T(8,128)(2,1)}, pred[64,384]{1,0:T(8,128)...) while((s32[]{:T(128)}, ...), condition=%wide.region_2.3_spmd, body=%wide.region_1.2_spmd.sunk | while | flops 204472320 | bytes 7342895 | solution.py:65
  251.2 2.6 fusion.30
  259.8 2.6 fusion.30
  268.4 2.6 fusion.30
  285.5 2.6 fusion.30
  302.6 2.6 fusion.30
  328.3 2.6 fusion.30
  345.5 2.6 fusion.30
  354.0 2.6 fusion.30
  362.6 2.6 fusion.30
  379.7 2.6 fusion.30
  396.8 2.6 fusion.30
  422.5 2.6 fusion.30
  431.0 2.6 fusion.30
  439.6 2.6 fusion.30
  456.7 2.6 fusion.30
  465.3 2.6 fusion.30
  482.4 2.6 fusion.30
  491.0 2.6 fusion.30
  499.5 2.6 fusion.30
  508.1 2.6 fusion.30
  516.7 2.6 fusion.30
  525.2 2.6 fusion.30
  533.8 2.6 fusion.30
  550.9 2.6 fusion.30
  576.6 2.6 fusion.30
  585.1 2.6 fusion.30
  593.7 2.6 fusion.30
  602.2 2.6 fusion.30
  610.8 2.6 fusion.30
  619.3 2.6 fusion.30
  636.4 2.6 fusion.30
  645.0 2.6 fusion.30
  653.6 2.6 fusion.30
  662.1 2.6 fusion.30
  670.7 2.6 fusion.30
  687.8 2.6 fusion.30
  704.9 2.6 fusion.30
  756.3 2.6 fusion.30
  773.4 2.6 fusion.30
  782.0 2.6 fusion.30
  790.5 2.6 fusion.30
  793.9 110.4 %reduce-scatter.2.cloned.1.call-done = bf16[4,128,1024]{1,2,0:T(8,128)(2,1)} async-done(((bf16[64,128,1024]{1,2,0:T(8,128)(2,1)}), bf16[4,128,1024]{1,2,0:T(8,128)(2,1)}) %reduce-scatter.2.cloned.1.call-update) | async-done | bytes 1048592 | tf_op jit(solution)/shard_map/reduce_scatter | solution.py:67
  907.3 3.3 fusion.17
  (450 shorter events, 325.9 us)
Async XLA Ops:
  6.5 1.6 copy-start
  6.5 1.9 copy-start.6
  6.5 123.7 %all-gather.3.cloned.1.call-start = ((), (), s32[]{:S(2)}) async-start(), calls=%async_computation.1 | async-start | bytes 28311552 | tf_op jit(solution)/shard_map/all_gather | solution.py:25
  7.3 238.8 %all-gather.5.cloned.1.call-start = ((), (), s32[]{:S(2)}) async-start(), calls=%async_computation.2 | async-start | bytes 17825792 | tf_op jit(solution)/shard_map/all_gather | solution.py:36
  10.2 1.3 copy-start.4
  10.2 1.5 copy-start.8
  10.2 1.5 copy-start.2
  10.2 2.3 copy-start.3
  11.5 892.9 %reduce-scatter.2.cloned.1.call-start = ((), (), s32[]{:S(2)}) async-start(), calls=%async_computation.3 | async-start | bytes 17825792 | tf_op jit(solution)/shard_map/reduce_scatter | solution.py:67
  793.9 113.4 %copy-start.7 = (bf16[4,128,1024]{2,1,0:T(8,128)(2,1)S(1)}, bf16[4,128,1024]{2,1,0:T(8,128)(2,1)}, u32[]{:S(2)}) copy-start(bf16[4,128,1024]{2,1,0:T(8,128)(2,1)} %param.11) | copy-start | bytes 3145732
  907.3 3.3 copy-start.5
  910.6 2.3 copy-start.1
Sparse Core Ops, SparseCore 0:
  9.0 121.1 all-gather.2
  132.4 113.6 all-gather.4
  794.0 110.2 reduce-scatter.1
where the time goes:
time: 927 us; the launch traced here: 919 us
  waiting for transfers between devices  320 us (35%)
  local copies, waits for them, and re-layouts  283 us (31%)
  matrix products  176 us (19%)
  loops' own time  125 us (13%)
  between operations  13.3 us (1%)
    dot_general x64, matrix products, one_tile(): jnp.einsum('hct,htd->chd', weights, value_rows, preferred_element_type=jn...  169 us
    another operation x1, loops' own time, per_device(): lax.map(one_tile, (q_tiles, slot_index, allowed, length_float))  125 us
    all_gather x1, waiting for transfers between devices, per_device(): cache_buffer = lax.all_gather(history_kv, 'cand', axis=0, tiled=True)  117 us
    reduce_scatter x1, waiting for transfers between devices, per_device(): lax.psum_scatter(partial_sums.astype(jnp.bfloat16), 'hist', scatter_dimen...  110 us
    dynamic_slice x64, local copies, waits for them, and re-layouts, one_tile(): key_rows = lax.dynamic_index_in_dim(key_heads, slot_one, 0, keepdims=False)  94.6 us
    all_gather x1, waiting for transfers between devices, per_device(): q_tiles = lax.all_gather(queries, 'hist', axis=0, tiled=True)  92.1 us
    dynamic_slice x192, local copies, waits for them, and re-layouts, per_device(): lax.map(one_tile, (q_tiles, slot_index, allowed, length_float))  76.7 us
    dynamic_update_slice x64, local copies, waits for them, and re-layouts, per_device(): lax.map(one_tile, (q_tiles, slot_index, allowed, length_float))  46.4 us
  transfers between devices with their start and end apart: 3, of which 3 were waited for; matrix products, arithmetic and copies ran while one was open for 3% of the time, Pallas kernels for 0%

commit v1 on v0

v1 whole, which is shorter than its diff:
```python
import functools

import jax
import jax.numpy as jnp
from jax import lax
from jax.experimental import pallas as pl
from jax.experimental.pallas import tpu as pltpu
from jax.sharding import PartitionSpec as P

DH = 128
CHUNKS = 2

norm_epsilon = 1e-05


def attend_kernel(order_ref, row_ref, q_ref, k_ref, v_ref, m_ref, o_ref, *, heads, span):
    del order_ref, row_ref
    half_scale = 0.5 / DH**0.5
    open_over_length = m_ref[0]
    for h in range(heads):
        cols = slice(h * DH, (h + 1) * DH)
        keys = k_ref[0, :, :, cols].reshape(span, DH)
        values = v_ref[0, :, :, cols].reshape(span, DH)
        half = (
            lax.dot_general(
                q_ref[0, :, cols],
                keys,
                (((1,), (1,)), ((), ())),
                preferred_element_type=jnp.float32,
            )
            * half_scale
        )
        weights = ((half + half * jnp.tanh(half)) * open_over_length).astype(jnp.bfloat16)
        out = jnp.dot(weights, values, preferred_element_type=jnp.float32)
        o_ref[0, :, cols] = out.astype(jnp.bfloat16)


def attend(order, sorted_rows, q_tiles, cache, open_over_length):
    tile_count, block_len, width = q_tiles.shape
    blocks_here = cache.shape[1]
    span = blocks_here * block_len
    kernel = functools.partial(attend_kernel, heads=width // DH, span=span)
    return pl.pallas_call(
        kernel,
        grid_spec=pltpu.PrefetchScalarGridSpec(
            num_scalar_prefetch=2,
            grid=(tile_count,),
            in_specs=[
                pl.BlockSpec((1, block_len, width), lambda i, order, rows: (order[i], 0, 0)),
                pl.BlockSpec((1, blocks_here, block_len, width), lambda i, order, rows: (rows[i], 0, 0, 0)),
                pl.BlockSpec((1, blocks_here, block_len, width), lambda i, order, rows: (rows[i], 0, 0, 1)),
                pl.BlockSpec((1, 1, span), lambda i, order, rows: (order[i], 0, 0)),
            ],
            out_specs=pl.BlockSpec((1, block_len, width), lambda i, order, rows: (order[i], 0, 0)),
        ),
        out_shape=jax.ShapeDtypeStruct(q_tiles.shape, jnp.bfloat16),
        cost_estimate=pl.CostEstimate(
            flops=4 * tile_count * block_len * span * width,
            bytes_accessed=4 * tile_count * block_len * width + 2 * cache.size,
            transcendentals=tile_count * block_len * span * (width // DH),
        ),
        compiler_params=pltpu.CompilerParams(vmem_limit_bytes=24 * 1024 * 1024),
    )(order, sorted_rows, q_tiles, cache, cache, open_over_length)


def per_device(cand_x, w_query, w_gate, w_out, history_kv, tile_user, user_row, hist_len, pattern):
    tiles_here, block_len, model_width = cand_x.shape
    blocks_here = history_kv.shape[1]
    span = blocks_here * block_len
    width = model_width // CHUNKS

    caches = []
    for c in range(CHUNKS):
        part = jnp.concatenate(
            [
                history_kv[..., c * width : (c + 1) * width],
                history_kv[..., model_width + c * width : model_width + (c + 1) * width],
            ],
            axis=-1,
        )
        caches.append(lax.all_gather(part, "cand", axis=0, tiled=True))

    flat_rows = cand_x.reshape(tiles_here * block_len, model_width)
    queries = jax.nn.silu(jnp.dot(flat_rows, w_query, preferred_element_type=jnp.float32)).astype(
        jnp.bfloat16
    )
    queries = queries.reshape(tiles_here, block_len, model_width)
    q_parts = [
        lax.all_gather(queries[..., c * width : (c + 1) * width], "hist", axis=0, tiled=True)
        for c in range(CHUNKS)
    ]
    gate_act = jax.nn.silu(jnp.dot(flat_rows, w_gate, preferred_element_type=jnp.float32)).astype(
        jnp.bfloat16
    )

    tile_count = tile_user.shape[0]
    rows_named = user_row[tile_user]
    lengths = hist_len[tile_user]
    tile_ids = jnp.arange(tile_count, dtype=jnp.int32)
    before = (rows_named[None, :] < rows_named[:, None]) | (
        (rows_named[None, :] == rows_named[:, None]) & (tile_ids[None, :] < tile_ids[:, None])
    )
    rank = jnp.sum(before.astype(jnp.int32), axis=1)
    placed = (rank[None, :] == tile_ids[:, None]).astype(jnp.int32)
    order = jnp.sum(placed * tile_ids[None, :], axis=1)
    sorted_rows = jnp.sum(placed * rows_named[None, :], axis=1)

    positions = lax.axis_index("hist") * span + jnp.arange(span, dtype=jnp.int32)
    block_open = jnp.broadcast_to(
        pattern[:, :, None], (tile_count, blocks_here, block_len)
    ).reshape(tile_count, span)
    allowed = (positions[None, :] < lengths[:, None]) & (block_open > 0)
    open_over_length = jnp.where(allowed, 1.0 / lengths.astype(jnp.float32)[:, None], 0.0)[:, None, :]

    sums = []
    for c in range(CHUNKS):
        partial = attend(order, sorted_rows, q_parts[c], caches[c], open_over_length)
        sums.append(lax.psum_scatter(partial, "hist", scatter_dimension=0, tiled=True))
    attention = jnp.concatenate(sums, axis=-1).astype(jnp.float32)
    attention = attention.reshape(tiles_here * block_len, model_width)
    mean_square = jnp.mean(attention * attention, axis=-1, keepdims=True)
    normed = attention * lax.rsqrt(mean_square + norm_epsilon)
    hidden = (normed * gate_act.astype(jnp.float32)).astype(jnp.bfloat16)
    mixed = jnp.dot(hidden, w_out, preferred_element_type=jnp.float32) + flat_rows.astype(
        jnp.float32
    )
    return mixed.astype(jnp.bfloat16).reshape(tiles_here, block_len, model_width)


def solution(mesh):
    return jax.shard_map(
        per_device,
        mesh=mesh,
        in_specs=(
            P(("cand", "hist"), None, None),
            P(),
            P(),
            P(),
            P("cand", "hist", None, None),
            P("cand"),
            P(),
            P(),
            P("cand", "hist"),
        ),
        out_specs=P(("cand", "hist"), None, None),
        check_vma=False,
    )
```

time: 927 us -> 488 us (0.53)
  local copies, waits for them, and re-layouts: 283 us -> 29 us
  matrix products: 176 us -> 9 us
  loops' own time: 125 us -> 0 us
  Pallas kernels: 0 us -> 115 us
    dynamic_slice x320 -> x0, local copies, waits for them, and re-layouts: 207 us -> none  [the longest x64 94.6 us: one_tile(): key_rows = lax.dynamic_index_in_dim(key_heads, slot_one, 0, keepdims=False)]
    dot_general x65 -> x0, matrix products: 173 us -> none  [the longest x64 169 us: one_tile(): jnp.einsum('hct,htd->chd', weights, value_rows, preferred_element_type=jn...]
    another operation x1 -> x0, loops' own time: 125 us -> none  [per_device(): lax.map(one_tile, (q_tiles, slot_index, allowed, length_float))]
    pallas_call x0 -> x2, Pallas kernels: none -> 115 us  [attend(): pl.pallas_call(kernel, grid_spec=pltpu.PrefetchScalarGridSpec(num_scalar_...]
    dynamic_update_slice x64 -> x0, local copies, waits for them, and re-layouts: 46.4 us -> none  [per_device(): lax.map(one_tile, (q_tiles, slot_index, allowed, length_float))]
    transpose x1 -> x0, local copies, waits for them, and re-layouts: 9.49 us -> none  [per_device(): key_heads = split_cache[:, :, 0].transpose(0, 2, 1, 3)]
    unnamed x20 -> x26, local copies, waits for them, and re-layouts: 15.6 us -> 24 us
    all_gather x2 -> x4, waiting for transfers between devices: 209 us -> 205 us  [the longest x2 134 us: per_device(): caches.append(lax.all_gather(part, 'cand', axis=0, tiled=True))]
  transfers between devices with their start and end apart: 3 -> 6, of which waited for: 3 -> 6; matrix products, arithmetic and copies ran while one was open for 3% -> 1% of each run, Pallas kernels for 0% -> 24%
where the time goes in v1:
time: 488 us; the launch traced here: 487 us
  waiting for transfers between devices  316 us (65%)
  Pallas kernels  115 us (24%)
  local copies, waits for them, and re-layouts  29 us (6%)
  between operations  13.7 us (3%)
  matrix products  9 us (2%)
    all_gather x2, waiting for transfers between devices, per_device(): caches.append(lax.all_gather(part, 'cand', axis=0, tiled=True))  134 us
    pallas_call x2, Pallas kernels, attend(): pl.pallas_call(kernel, grid_spec=pltpu.PrefetchScalarGridSpec(num_scalar_...  115 us
    reduce_scatter x2, waiting for transfers between devices, per_device(): lax.psum_scatter(partial, 'hist', scatter_dimension=0, tiled=True)  110 us
    all_gather x2, waiting for transfers between devices, per_device(): lax.all_gather(queries[..., c * width:(c + 1) * width], 'hist', axis=0, t...  71.7 us
    unnamed x26, local copies, waits for them, and re-layouts  24 us
  transfers between devices with their start and end apart: 6, of which 6 were waited for; matrix products, arithmetic and copies ran while one was open for 1% of the time, Pallas kernels for 24%

profile of v1, /device:TPU:24, one launch (start us, length us, event | category | flops | bytes accessed | tf_op | source)
XLA Modules:
  0.0 487.3 jit_solution(10648020460692982431)
XLA Ops:
  6.5 1.6 copy-done
  8.1 2.7 multiply_convert_fusion.1
  10.8 1.1 fusion.11
  11.9 0.0 all-gather.5.cloned.1.call-update
  11.9 0.0 all-gather.7.cloned.1.call-start
  12.0 2.1 fusion.10
  14.1 1.3 pad_maximum_fusion
  15.4 0.0 all-gather.7.cloned.1.call-update
  15.4 0.0 all-gather.9.cloned.1.call-start
  15.5 0.7 all-gather.9.cloned.1.call-update
  16.2 0.0 all-gather.11.cloned.1.call-start
  16.2 0.0 copy-start.12
  16.2 0.0 copy-start.8
  16.2 0.0 copy-start.9
  16.2 1.4 pad_maximum_fusion.1
  17.6 0.0 all-gather.11.cloned.1.call-update
  17.6 0.0 reduce-scatter.3.cloned.1.call-start
  17.7 0.8 gather_fusion
  18.5 0.0 copy-done.9
  18.5 0.8 gather_fusion.1
  19.3 0.1 copy.15
  19.4 0.1 broadcast_in_dim.13
  19.6 0.1 gt.20
  19.7 0.2 convert_reduce_fusion
  19.8 0.1 select_reduce_fusion
  20.0 0.2 and_select_fusion.m_ref
  20.2 64.8 %all-gather.5.cloned.1.call-done.q_ref = bf16[64,128,512]{2,1,0:T(8,128)(2,1)} async-done(((bf16[4,128,512]{2,1,0:T(8,128)(2,1)}), bf16[64,128,512]{2,1,0:T(8,128)(2,1)}) %all-gather.5.cloned.1.call-update) | async-done | bytes 8388624 | tf_op jit(solution)/shard_map/all_gather | solution.py:89
  85.1 66.8 %all-gather.7.cloned.1.call-done.k_ref.v_ref = bf16[16,3,128,1024]{3,2,1,0:T(8,128)(2,1)} async-done(((bf16[2,3,128,1024]{3,2,1,0:T(8,128)(2,1)}), bf16[16,3,128,1024]{3,2,1,0:T(8,128)(2,1)}) %all-gather.7.cloned.1.call-update) | async-done | bytes 12582928 | tf_op jit(solution)/shard_map/all_gather | solution.py:81
  151.9 4.6 copy-done.2
  156.5 3.4 copy-done.6
  159.8 57.4 %shard_map.91 = bf16[64,128,512]{2,1,0:T(8,128)(2,1)S(1)} custom-call(s32[64]{0:T(128)S(1)} %get-tuple-element.6.order_ref, s32[64]{0:T(128)S(1)} %get-tuple-element.5.row_ref, bf16[64,128,512]{2,1,0:T(8,128)(2,1)S(1)} %copy-done.6, bf16[16,3,128,1024]{3,2,1,0:T(8,128)(2,1)S(1)} %copy-done.2, bf16[16,3,128,1024]{3,2,1,0:T(8,128)(2,1)S(1)} %copy-done.2, ...), custom_call_target="tpu_custom_call" | custom-call | flops 6442450944 | bytes 29360128 | tf_op jit(solution)/shard_map/pallas_call | solution.py:43
  217.2 3.2 copy-done.4
  220.4 0.0 reduce-scatter.3.cloned.1.call-update
  220.5 0.0 reduce-scatter.5.cloned.1.call-start
  220.5 6.8 %all-gather.9.cloned.1.call-done.q_ref = bf16[64,128,512]{2,1,0:T(8,128)(2,1)} async-done(((bf16[4,128,512]{2,1,0:T(8,128)(2,1)}), bf16[64,128,512]{2,1,0:T(8,128)(2,1)}) %all-gather.9.cloned.1.call-update) | async-done | bytes 8388624 | tf_op jit(solution)/shard_map/all_gather | solution.py:89
  227.3 66.7 %all-gather.11.cloned.1.call-done.k_ref.v_ref = bf16[16,3,128,1024]{3,2,1,0:T(8,128)(2,1)} async-done(((bf16[2,3,128,1024]{3,2,1,0:T(8,128)(2,1)}), bf16[16,3,128,1024]{3,2,1,0:T(8,128)(2,1)}) %all-gather.11.cloned.1.call-update) | async-done | bytes 12582928 | tf_op jit(solution)/shard_map/all_gather | solution.py:81
  294.1 4.6 copy-done.3
  298.6 3.4 copy-done.7
  302.0 57.4 %shard_map.92 = bf16[64,128,512]{2,1,0:T(8,128)(2,1)S(1)} custom-call(s32[64]{0:T(128)S(1)} %get-tuple-element.6.order_ref, s32[64]{0:T(128)S(1)} %get-tuple-element.5.row_ref, bf16[64,128,512]{2,1,0:T(8,128)(2,1)S(1)} %copy-done.7, bf16[16,3,128,1024]{3,2,1,0:T(8,128)(2,1)S(1)} %copy-done.3, bf16[16,3,128,1024]{3,2,1,0:T(8,128)(2,1)S(1)} %copy-done.3, ...), custom_call_target="tpu_custom_call" | custom-call | flops 6442450944 | bytes 29360128 | tf_op jit(solution)/shard_map/pallas_call | solution.py:43
  359.4 0.0 copy-start.5
  359.4 3.2 copy-done.5
  362.6 0.0 reduce-scatter.5.cloned.1.call-update
  362.6 22.2 %reduce-scatter.3.cloned.1.call-done = bf16[4,128,512]{2,1,0:T(8,128)(2,1)} async-done(((bf16[64,128,512]{2,1,0:T(8,128)(2,1)}), bf16[4,128,512]{2,1,0:T(8,128)(2,1)}) %reduce-scatter.3.cloned.1.call-update) | async-done | bytes 524304 | tf_op jit(solution)/shard_map/reduce_scatter | solution.py:118
  384.9 87.8 %reduce-scatter.5.cloned.1.call-done = bf16[4,128,512]{2,1,0:T(8,128)(2,1)} async-done(((bf16[64,128,512]{2,1,0:T(8,128)(2,1)}), bf16[4,128,512]{2,1,0:T(8,128)(2,1)}) %reduce-scatter.5.cloned.1.call-update) | async-done | bytes 524304 | tf_op jit(solution)/shard_map/reduce_scatter | solution.py:118
  472.7 1.5 fusion
  474.2 0.0 copy-start.1
  474.2 6.3 %add_convert_fusion = bf16[512,1024]{1,0:T(8,128)(2,1)} fusion(bf16[512,1024]{1,0:T(8,128)(2,1)S(1)} %bitcast.16, bf16[1024,1024]{1,0:T(8,128)(2,1)} %param.12, f32[512]{0:T(512)S(1)} %add_rsqrt_fusion, bf16[512,512]{1,0:T(8,128)(2,1)} %bitcast.14, bf16[512,512]{1,0:T(8,128)(2,1)} %bitcast.12, bf16[1024,1024]{1,0:T(8,128)(2,1)} %param.11), kind=kOutput, calls=%fused_computation.7 | convolution fusion | flops 2155872256 | bytes 7342080 | tf_op jit(solution)/shard_map/dot_general | solution.py:124
  480.5 0.0 copy-done.1
  (19 shorter events, 0.1 us)
Async XLA Ops:
  6.5 1.6 copy-start
  6.5 78.5 %all-gather.5.cloned.1.call-start = ((), (), s32[]{:S(2)}) async-start(), calls=%async_computation.2 | async-start | bytes 8912896 | tf_op jit(solution)/shard_map/all_gather | solution.py:89
  11.9 139.9 %all-gather.7.cloned.1.call-start = ((), (), s32[]{:S(2)}) async-start(), calls=%async_computation.3 | async-start | bytes 14155776 | tf_op jit(solution)/shard_map/all_gather | solution.py:81
  15.4 211.9 %all-gather.9.cloned.1.call-start = ((), (), s32[]{:S(2)}) async-start(), calls=%async_computation.5 | async-start | bytes 8912896 | tf_op jit(solution)/shard_map/all_gather | solution.py:89
  16.2 277.9 %all-gather.11.cloned.1.call-start = ((), (), s32[]{:S(2)}) async-start(), calls=%async_computation.6 | async-start | bytes 14155776 | tf_op jit(solution)/shard_map/all_gather | solution.py:81
  16.2 1.5 copy-start.12
  16.2 1.5 copy-start.8
  16.2 2.3 copy-start.9
  17.6 1.7 copy-start.10
  17.6 367.2 %reduce-scatter.3.cloned.1.call-start = ((), (), s32[]{:S(2)}) async-start(), calls=%async_computation.4 | async-start | bytes 8912896 | tf_op jit(solution)/shard_map/reduce_scatter | solution.py:118
  151.9 4.6 copy-start.2
  156.5 3.4 copy-start.6
  217.2 3.2 copy-start.4
  220.5 252.2 %reduce-scatter.5.cloned.1.call-start = ((), (), s32[]{:S(2)}) async-start(), calls=%async_computation.7 | async-start | bytes 8912896 | tf_op jit(solution)/shard_map/reduce_scatter | solution.py:118
  294.1 4.6 copy-start.3
  298.6 3.4 copy-start.7
  359.4 3.2 copy-start.5
  362.6 111.6 %copy-start.11 = (bf16[4,128,1024]{2,1,0:T(8,128)(2,1)S(1)}, bf16[4,128,1024]{2,1,0:T(8,128)(2,1)}, u32[]{:S(2)}) copy-start(bf16[4,128,1024]{2,1,0:T(8,128)(2,1)} %param.9) | copy-start | bytes 3145732
  474.2 6.3 %copy-start.1 = (bf16[1024,1024]{1,0:T(8,128)(2,1)S(1)}, bf16[1024,1024]{1,0:T(8,128)(2,1)}, u32[]{:S(2)}) copy-start(bf16[1024,1024]{1,0:T(8,128)(2,1)} %param.10) | copy-start | bytes 6291460
Sparse Core Ops, SparseCore 0:
  12.1 72.9 all-gather.4
  86.8 65.0 all-gather.6
  154.0 73.2 all-gather.8
  228.9 65.1 all-gather.10
  297.3 87.5 reduce-scatter.2
  388.1 84.5 reduce-scatter.4
